TPU v7x, 32 devices: a whole 2x2x4 slice. The times are simulated.
32 devices in a mesh: groups: 2 (over x), morton: 16 (over z, y, core).
Axes of the slice: x: 2, y: 2, z: 4, core: 2. Of those that a mesh axis runs over, the one named last changes fastest.
Arguments:
- features: bfloat16 [64, 512, 128], P(('groups', 'morton')), parts along dimension 0, may hold values from -6 to 6
- cotangent: bfloat16 [64, 512, 128], P(('groups', 'morton')), parts along dimension 0, may hold values from -6 to 6
- coarse: bfloat16 [128, 512, 256], P(('groups', 'morton')), parts along dimension 0, may hold values from -6 to 6
- kernel: bfloat16 [27, 128, 128], replicated, may hold values from -0.109375 to 0.109375
- coarse_weight: bfloat16 [256, 128], replicated, may hold values from -0.375 to 0.375
- brick_links: int32 [64, 27], P(('groups', 'morton')), parts along dimension 0, may hold values from -1 to 31, as said below
- parent_slot: int32 [64], P(('groups', 'morton')), parts along dimension 0, may hold values from 0 to 508, as said below
Outputs:
- grad_input: bfloat16 [64, 512, 128], P(('groups', 'morton')), parts along dimension 0
- grad_kernel: float32 [54, 128, 128], P('groups'), parts along dimension 0
- grad_coarse_weight: float32 [512, 128], P('groups'), parts along dimension 0
There are 2 independent parts, one for each index of `groups`. A program takes and returns all parts, laid end to end along the dimension named above; an argument that names none is the same for every part. Nothing has to cross between parts.
Inputs may be any that keep to these rules, and one draw needn't show every extreme that they name: `brick_links`: entries are -1 or a brick index; links are symmetric. An index outside b's Morton range of 2 bricks lies in the range just before it, at an offset with dz = -1, or just after it, at an offset with dz = 1. `parent_slot`: 8 p + o with o = 4 oz + 2 oy + ox; p // 4 equals b // 2.
All inputs are finite; a program needn't handle non-finite values.
Results may differ from a plain program's by a relative error of at most 0.001.
The roundings to bfloat16 on the way count: a program that leaves them out, or rounds other values in their place, can miss the bound.
Values may be sent and summed in bfloat16 or wider, within the bound.
A program may use at most 64 MiB of HBM per device.

v0:
```python
import jax
import jax.numpy as jnp
from jax import lax
from jax.sharding import PartitionSpec as P

SPANS = ((7, 8), (0, 8), (0, 1))


def padded_2(cells, sides, width):
    for axis, dim in sides:
        count = lax.axis_size(axis)
        ends = count - 1
        head = lax.slice_in_dim(cells, 0, width, axis=dim)
        tail = lax.slice_in_dim(cells, cells.shape[dim] - width, cells.shape[dim], axis=dim)
        cells = jnp.concatenate(
            [
                lax.ppermute(tail, axis, [(i, (i + 1) % count) for i in range(ends)]),
                cells,
                lax.ppermute(head, axis, [((i + 1) % count, i) for i in range(ends)]),
            ],
            axis=dim,
        )
    return cells


def build_padded(source, positions):
    planes = []
    for z_off in range(3):
        rows_list = []
        for y_off in range(3):
            pieces = []
            for x_off in range(3):
                zlo, zhi = SPANS[z_off]
                ylo, yhi = SPANS[y_off]
                xlo, xhi = SPANS[x_off]
                slab = source[:, zlo:zhi, ylo:yhi, xlo:xhi, :]
                pieces.append(slab[positions[:, z_off * 9 + y_off * 3 + x_off]])
            rows_list.append(jnp.concatenate(pieces, axis=3))
        planes.append(jnp.concatenate(rows_list, axis=2))
    return jnp.concatenate(planes, axis=1)


def convolve(padded, kernel):
    channels = kernel.shape[-1]
    grouped = kernel.reshape(9, 3 * channels, channels)
    summed = jnp.zeros((padded.shape[0] * 512, channels), jnp.float32)
    for z_off in range(3):
        for y_off in range(3):
            window = jnp.concatenate(
                [
                    padded[:, z_off : z_off + 8, y_off : y_off + 8, x_off : x_off + 8, :]
                    for x_off in range(3)
                ],
                axis=-1,
            )
            summed = summed + jnp.dot(
                window.reshape(-1, 3 * channels),
                grouped[z_off * 3 + y_off],
                preferred_element_type=jnp.float32,
            )
    return summed


def convolve_back(padded, kernel):
    channels = kernel.shape[-1]
    flipped = jnp.swapaxes(kernel, 1, 2).reshape(9, 3 * channels, channels)
    summed = jnp.zeros((padded.shape[0] * 512, channels), jnp.float32)
    for z_off in range(3):
        for y_off in range(3):
            window = jnp.concatenate(
                [
                    padded[
                        :, 2 - z_off : 10 - z_off, 2 - y_off : 10 - y_off, 2 - x_off : 10 - x_off, :
                    ]
                    for x_off in range(3)
                ],
                axis=-1,
            )
            summed = summed + jnp.dot(
                window.reshape(-1, 3 * channels),
                flipped[z_off * 3 + y_off],
                preferred_element_type=jnp.float32,
            )
    return summed


def weight_terms(padded, output_gradient):
    channels = output_gradient.shape[-1]
    pieces = []
    for z_off in range(3):
        for y_off in range(3):
            window = jnp.concatenate(
                [
                    padded[:, z_off : z_off + 8, y_off : y_off + 8, x_off : x_off + 8, :]
                    for x_off in range(3)
                ],
                axis=-1,
            )
            term = lax.dot_general(
                window.reshape(-1, 3 * channels),
                output_gradient,
                (((0,), (0,)), ((), ())),
                preferred_element_type=jnp.float32,
            )
            pieces.append(term.reshape(3, channels, channels))
    return jnp.concatenate(pieces, axis=0)


def octant_layout(coarse):
    brick_list, cells, chans = coarse.shape
    shaped = coarse.reshape(brick_list, 2, 4, 2, 4, 2, 4, chans).transpose(0, 1, 3, 5, 2, 4, 6, 7)
    return shaped.reshape(brick_list * 8, 64, chans)


def upsample(brick_region):
    brick_list, cells, chans = brick_region.shape
    shaped = brick_region.reshape(brick_list, 4, 1, 4, 1, 4, 1, chans)
    return jnp.broadcast_to(shaped, (brick_list, 4, 2, 4, 2, 4, 2, chans)).reshape(
        brick_list * 512, chans
    )


def reduce_resolution(gradient_rows, brick_list):
    chans = gradient_rows.shape[-1]
    return (
        gradient_rows.astype(jnp.float32)
        .reshape(brick_list, 4, 2, 4, 2, 4, 2, chans)
        .sum(axis=(2, 4, 6))
        .reshape(brick_list * 64, chans)
    )


def from_bricks(wide, cells_here):
    brick_list = cells_here.shape[0]
    spare = jnp.zeros((1,) + cells_here.shape[1:], cells_here.dtype)
    return jnp.concatenate([wide.reshape((3 * brick_list,) + cells_here.shape[1:]), spare], axis=0)


def local(features, cotangent, coarse, kernel, coarse_weight, brick_links, parent_slot):
    brick_list = features.shape[0]
    channels = features.shape[2]
    coarse_chans = coarse.shape[2]
    device = lax.axis_index("morton")
    cells_here = features.reshape(brick_list, 8, 8, 8, channels)
    positions = jnp.where(brick_links < 0, 3 * brick_list, brick_links - (device - 1) * brick_list)
    wide = padded_2(features, (("morton", 0),), brick_list)
    source = from_bricks(wide, cells_here)
    padded = build_padded(source, positions)
    parents = parent_slot - device * coarse.shape[0] * 8
    coarse_oct = octant_layout(coarse)
    projected = jnp.dot(
        coarse_oct.reshape(-1, coarse_chans), coarse_weight, preferred_element_type=jnp.float32
    ).reshape(-1, 64, channels)
    summed_in = convolve(padded, kernel) + upsample(projected[parents])
    sigmoid_at = jax.nn.sigmoid(summed_in)
    grads = cotangent.reshape(-1, channels).astype(jnp.float32)
    output_gradient = (grads * sigmoid_at * (1.0 + summed_in * (1.0 - sigmoid_at))).astype(
        jnp.bfloat16
    )
    slope_cells = output_gradient.reshape(brick_list, 8, 8, 8, channels)
    slope_wide = padded_2(
        output_gradient.reshape(brick_list, 512, channels), (("morton", 0),), brick_list
    )
    slope_source = from_bricks(slope_wide, slope_cells)
    kernel_term = weight_terms(padded, output_gradient)
    brick_region = coarse_oct[parents].reshape(-1, coarse_chans).astype(jnp.float32)
    coarse_contribution = lax.dot_general(
        brick_region,
        reduce_resolution(output_gradient, brick_list),
        (((0,), (0,)), ((), ())),
        precision=lax.Precision.HIGHEST,
        preferred_element_type=jnp.float32,
    )
    factor = (brick_list * 512 * lax.axis_size("morton")) ** (-0.5)
    kernel_sum, coarse_sum = lax.psum((kernel_term, coarse_contribution), "morton")
    kernel_out = kernel_sum * factor
    coarse_out = coarse_sum * factor
    grad_rows = convolve_back(build_padded(slope_source, positions), kernel).astype(jnp.bfloat16)
    return (grad_rows.reshape(brick_list, 512, channels), kernel_out, coarse_out)


def solution(mesh):
    return jax.shard_map(
        local,
        mesh=mesh,
        in_specs=(
            P(("groups", "morton"), None, None),
            P(("groups", "morton"), None, None),
            P(("groups", "morton"), None, None),
            P(),
            P(),
            P(("groups", "morton"), None),
            P(("groups", "morton")),
        ),
        out_specs=(P(("groups", "morton"), None, None), P("groups", None, None), P("groups", None)),
        check_vma=False,
    )
```

profile of v0, /device:TPU:0, one launch (start us, length us, event | category | flops | bytes accessed | tf_op | source)
XLA Modules:
  0.0 203.1 jit_solution(16045149348012717541)
XLA Ops:
  7.2 2.5 %collective-permute-start = (bf16[2,512,128]{2,1,0:T(8,128)(2,1)}, bf16[2,512,128]{2,1,0:T(8,128)(2,1)S(1)}, u32[]{:S(2)}, u32[]{:S(2)}) collective-permute-start(bf16[2,512,128]{2,1,0:T(8,128)(2,1)} %param.7), channel_id=1, source_target_pairs={{0,1},{1,2},{2,3},{3,4},{4,5},{5,6},{6,7},{7,8},{8,9},{9,10},{10,1... | collective-permute-start | bytes 786440 | tf_op jit(solution)/shard_map/ppermute | solution.py:17
  9.8 1.3 collective-permute-start.1
  12.5 2.2 %fusion.56 = (bf16[3,128,128]{2,1,0:T(8,128)(2,1)}, bf16[3,128,128]{2,1,0:T(8,128)(2,1)}, bf16[3,128,128]{2,1,0:T(8,128)(2,1)}, bf16[3,128,128]{2,1,0:T(8,128)(2...) fusion(bf16[27,128,128]{2,1,0:T(8,128)(2,1)} %param.10), kind=kLoop, calls=%fused_computation.284 | loop fusion | bytes 1769472 | tf_op jit(solution)/shard_map/slice | solution.py:58
  18.5 1.4 fusion.22
  20.5 1.3 copy.160
  21.8 1.2 gather_fusion.55
  23.0 1.8 gather_fusion.27
  25.8 1.0 pad_maximum_fusion.4
  42.2 1.3 fusion.59
  61.6 5.9 %collective-permute-start.2 = (bf16[2,512,128]{2,1,0:T(8,128)(2,1)S(1)}, bf16[2,512,128]{2,1,0:T(8,128)(2,1)}, u32[]{:S(2)}, u32[]{:S(2)}) collective-permute-start(bf16[2,512,128]{2,1,0:T(8,128)(2,1)S(1)} %bitcast.341), channel_id=1, source_target_pairs={{0,1},{1,2},{2,3},{3,4},{4,5},{5,6},{6,7},{7,8},{8,9},{9,10},{10,1... | collective-permute-start | bytes 786440 | tf_op jit(solution)/shard_map/ppermute | solution.py:17
  67.5 1.5 collective-permute-start.3
  68.9 1.2 copy.175
  70.2 2.3 %convolution_dynamic-update-slice_fusion.8 = f32[27,128,128]{2,1,0:T(8,128)} fusion(bf16[3,128,1024]{2,1,0:T(8,128)(2,1)} %bitcast.374, bf16[1024,128]{1,0:T(8,128)(2,1)S(1)} %fusion.12), kind=kOutput, calls=%fused_computation.86 | convolution fusion | flops 100663296 | bytes 1245184 | tf_op jit(solution)/shard_map/dot_general | solution.py:99
  72.4 2.3 %copy.176 = bf16[384,1024]{1,0:T(8,128)(2,1)} copy(bf16[384,1024]{0,1:T(8,128)(2,1)} %bitcast.360) | data formatting | bytes 1572864 | tf_op jit(solution)/shard_map/dot_general | solution.py:99
  74.7 1.2 copy.177
  75.9 2.4 %copy.178 = bf16[384,1024]{1,0:T(8,128)(2,1)} copy(bf16[384,1024]{0,1:T(8,128)(2,1)} %bitcast.356) | data formatting | bytes 1572864 | tf_op jit(solution)/shard_map/dot_general | solution.py:99
  78.3 1.2 copy.179
  79.7 1.2 copy.181
  82.1 1.0 convolution_dynamic-update-slice_fusion.7
  83.1 1.0 convolution_dynamic-update-slice_fusion.6
  84.2 1.0 convolution_dynamic-update-slice_fusion.5
  85.2 1.0 convolution_dynamic-update-slice_fusion.4
  86.3 1.0 convolution_dynamic-update-slice_fusion.3
  87.3 1.0 convolution_dynamic-update-slice_fusion.2
  88.4 1.0 convolution_dynamic-update-slice_fusion.1
  90.8 1.1 convolution_dynamic-update-slice_fusion
  91.9 1.1 copy.134
  93.1 1.1 copy.136
  111.3 1.2 fusion.57
  132.5 1.1 fusion.4
  133.6 59.1 %all-reduce.5.cloned.1.call-done = (f32[27,128,128]{2,1,0:T(8,128)}, f32[256,128]{1,0:T(8,128)}) async-done(((f32[27,128,128]{2,1,0:T(8,128)}, f32[256,128]{1,0:T(8,128)}), (f32[27,128,128]{2,1,0:T(8,128)}, f32[256,128]{1,0:T(8,128)})) %all-reduce.5.cloned.1.call-update) | async-done | bytes 1900560 | tf_op jit(solution)/shard_map/psum | solution.py:175
  192.6 2.9 %broadcast_multiply_fusion = f32[27,128,128]{2,1,0:T(8,128)} fusion(f32[27,128,128]{2,1,0:T(8,128)} %get-tuple-element.30), kind=kLoop, calls=%fused_computation.89 | loop fusion | flops 442368 | bytes 3538944 | tf_op jit(solution)/shard_map/mul | solution.py:176
  (404 shorter events, 79.2 us)
Async XLA Ops:
  7.2 11.4 %copy-start = (bf16[256,128]{1,0:T(8,128)(2,1)S(1)}, bf16[256,128]{1,0:T(8,128)(2,1)}, u32[]{:S(2)}) copy-start(bf16[256,128]{1,0:T(8,128)(2,1)} %param.11) | copy-start | bytes 196612
  7.2 7.5 %copy-start.16 = (bf16[4,512,256]{2,1,0:T(8,128)(2,1)S(1)}, bf16[4,512,256]{2,1,0:T(8,128)(2,1)}, u32[]{:S(2)}) copy-start(bf16[4,512,256]{2,1,0:T(8,128)(2,1)} %param.9) | copy-start | bytes 3145732
  7.2 185.4 %all-reduce.5.cloned.1.call-start = ((), (), s32[]{:S(2)}) async-start(), calls=%async_computation | async-start | bytes 3801088 | tf_op jit(solution)/shard_map/psum | solution.py:175
  7.2 18.5 %collective-permute-start = (bf16[2,512,128]{2,1,0:T(8,128)(2,1)}, bf16[2,512,128]{2,1,0:T(8,128)(2,1)S(1)}, u32[]{:S(2)}, u32[]{:S(2)}) collective-permute-start(bf16[2,512,128]{2,1,0:T(8,128)(2,1)} %param.7), channel_id=1, source_target_pairs={{0,1},{1,2},{2,3},{3,4},{4,5},{5,6},{6,7},{7,8},{8,9},{9,10},{10,1... | collective-permute-start | bytes 786440 | tf_op jit(solution)/shard_map/ppermute | solution.py:17
  9.8 16.0 %collective-permute-start.1 = (bf16[2,512,128]{2,1,0:T(8,128)(2,1)}, bf16[2,512,128]{2,1,0:T(8,128)(2,1)}, u32[]{:S(2)}, u32[]{:S(2)}) collective-permute-start(bf16[2,512,128]{2,1,0:T(8,128)(2,1)} %param.7), channel_id=1, source_target_pairs={{1,0},{2,1},{3,2},{4,3},{5,4},{6,5},{7,6},{8,7},{9,8},{10,9},{11,1... | collective-permute-start | bytes 786440 | tf_op jit(solution)/shard_map/ppermute | solution.py:19
  15.8 4.7 %copy-start.8 = (bf16[27,128,128]{2,1,0:T(8,128)(2,1)S(1)}, bf16[27,128,128]{2,1,0:T(8,128)(2,1)}, u32[]{:S(2)}) copy-start(bf16[27,128,128]{2,1,0:T(8,128)(2,1)} %param.10) | copy-start | bytes 2654212
  16.4 13.3 %copy-start.80 = (s32[1024]{0:T(1024)}, s32[1024]{0:T(1024)S(1)}, u32[]{:S(2)}) copy-start(s32[1024]{0:T(1024)S(1)} %get-tuple-element.172) | copy-start | bytes 12292
  16.4 13.8 %copy-start.81 = (s32[1024]{0:T(1024)}, s32[1024]{0:T(1024)S(1)}, u32[]{:S(2)}) copy-start(s32[1024]{0:T(1024)S(1)} %get-tuple-element.170) | copy-start | bytes 12292
  16.4 20.6 %copy-start.67 = (s32[1024]{0:T(1024)}, s32[1024]{0:T(1024)S(1)}, u32[]{:S(2)}) copy-start(s32[1024]{0:T(1024)S(1)} %get-tuple-element.171) | copy-start | bytes 12292
  16.4 14.4 %copy-start.72 = (s32[1024]{0:T(1024)}, s32[1024]{0:T(1024)S(1)}, u32[]{:S(2)}) copy-start(s32[1024]{0:T(1024)S(1)} %get-tuple-element.163) | copy-start | bytes 12292
  16.5 22.4 %copy-start.73 = (s32[1024]{0:T(1024)}, s32[1024]{0:T(1024)S(1)}, u32[]{:S(2)}) copy-start(s32[1024]{0:T(1024)S(1)} %get-tuple-element.162) | copy-start | bytes 12292
  16.5 15.0 %copy-start.71 = (s32[1024]{0:T(1024)}, s32[1024]{0:T(1024)S(1)}, u32[]{:S(2)}) copy-start(s32[1024]{0:T(1024)S(1)} %get-tuple-element.161) | copy-start | bytes 12292
  16.5 18.7 %copy-start.76 = (s32[1024]{0:T(1024)}, s32[1024]{0:T(1024)S(1)}, u32[]{:S(2)}) copy-start(s32[1024]{0:T(1024)S(1)} %get-tuple-element.160) | copy-start | bytes 12292
  16.5 15.5 %copy-start.70 = (s32[1024]{0:T(1024)}, s32[1024]{0:T(1024)S(1)}, u32[]{:S(2)}) copy-start(s32[1024]{0:T(1024)S(1)} %get-tuple-element.157) | copy-start | bytes 12292
  16.5 22.9 %copy-start.74 = (s32[1024]{0:T(1024)}, s32[1024]{0:T(1024)S(1)}, u32[]{:S(2)}) copy-start(s32[1024]{0:T(1024)S(1)} %get-tuple-element.156) | copy-start | bytes 12292
  16.6 16.1 %copy-start.79 = (s32[1024]{0:T(1024)}, s32[1024]{0:T(1024)S(1)}, u32[]{:S(2)}) copy-start(s32[1024]{0:T(1024)S(1)} %get-tuple-element.166) | copy-start | bytes 12292
  16.6 17.9 %copy-start.66 = (s32[1024]{0:T(1024)}, s32[1024]{0:T(1024)S(1)}, u32[]{:S(2)}) copy-start(s32[1024]{0:T(1024)S(1)} %get-tuple-element.167) | copy-start | bytes 12292
  16.6 16.6 %copy-start.78 = (s32[1024]{0:T(1024)}, s32[1024]{0:T(1024)S(1)}, u32[]{:S(2)}) copy-start(s32[1024]{0:T(1024)S(1)} %get-tuple-element.164) | copy-start | bytes 12292
  16.6 21.7 %copy-start.65 = (s32[1024]{0:T(1024)}, s32[1024]{0:T(1024)S(1)}, u32[]{:S(2)}) copy-start(s32[1024]{0:T(1024)S(1)} %get-tuple-element.165) | copy-start | bytes 12292
  16.6 17.2 %copy-start.68 = (s32[1024]{0:T(1024)}, s32[1024]{0:T(1024)S(1)}, u32[]{:S(2)}) copy-start(s32[1024]{0:T(1024)S(1)} %get-tuple-element.169) | copy-start | bytes 12292
  16.6 21.0 %copy-start.69 = (s32[1024]{0:T(1024)}, s32[1024]{0:T(1024)S(1)}, u32[]{:S(2)}) copy-start(s32[1024]{0:T(1024)S(1)} %get-tuple-element.168) | copy-start | bytes 12292
  16.7 19.1 %copy-start.77 = (s32[1024]{0:T(1024)}, s32[1024]{0:T(1024)S(1)}, u32[]{:S(2)}) copy-start(s32[1024]{0:T(1024)S(1)} %get-tuple-element.158) | copy-start | bytes 12292
  16.7 23.3 %copy-start.64 = (s32[1024]{0:T(1024)}, s32[1024]{0:T(1024)S(1)}, u32[]{:S(2)}) copy-start(s32[1024]{0:T(1024)S(1)} %get-tuple-element.159) | copy-start | bytes 12292
  16.7 19.7 %copy-start.75 = (s32[1024]{0:T(1024)}, s32[1024]{0:T(1024)S(1)}, u32[]{:S(2)}) copy-start(s32[1024]{0:T(1024)S(1)} %get-tuple-element.155) | copy-start | bytes 12292
  20.5 5.2 %copy-start.53 = (bf16[2,512,128]{2,1,0:T(8,128)(2,1)S(1)}, bf16[2,512,128]{2,1,0:T(8,128)(2,1)}, u32[]{:S(2)}) copy-start(bf16[2,512,128]{2,1,0:T(8,128)(2,1)} %param.7) | copy-start | bytes 786436
  43.5 4.9 %copy-start.58 = (bf16[7,8,128]{2,0,1:T(8,128)(2,1)S(1)}, bf16[7,8,128]{2,0,1:T(8,128)(2,1)}, u32[]{:S(2)}) copy-start(bf16[7,8,128]{2,0,1:T(8,128)(2,1)} %get-tuple-element.47) | copy-start | bytes 43012
  43.5 5.6 %copy-start.57 = (bf16[7,8,128]{2,0,1:T(8,128)(2,1)S(1)}, bf16[7,8,128]{2,0,1:T(8,128)(2,1)}, u32[]{:S(2)}) copy-start(bf16[7,8,128]{2,0,1:T(8,128)(2,1)} %get-tuple-element.46) | copy-start | bytes 43012
  43.6 6.3 %copy-start.56 = (bf16[7,8,128]{2,0,1:T(8,128)(2,1)S(1)}, bf16[7,8,128]{2,0,1:T(8,128)(2,1)}, u32[]{:S(2)}) copy-start(bf16[7,8,128]{2,0,1:T(8,128)(2,1)} %get-tuple-element.42) | copy-start | bytes 43012
  54.3 6.4 %copy-start.9 = (bf16[2,8,8,8,384]{4,3,2,1,0:T(8,128)(2,1)}, bf16[2,8,8,8,384]{4,3,2,1,0:T(8,128)(2,1)S(1)}, u32[]{:S(2)}) copy-start(bf16[2,8,8,8,384]{4,3,2,1,0:T(8,128)(2,1)S(1)} %pad_maximum_fusion.12) | copy-start | bytes 2359300
  61.6 30.3 %collective-permute-start.2 = (bf16[2,512,128]{2,1,0:T(8,128)(2,1)S(1)}, bf16[2,512,128]{2,1,0:T(8,128)(2,1)}, u32[]{:S(2)}, u32[]{:S(2)}) collective-permute-start(bf16[2,512,128]{2,1,0:T(8,128)(2,1)S(1)} %bitcast.341), channel_id=1, source_target_pairs={{0,1},{1,2},{2,3},{3,4},{4,5},{5,6},{6,7},{7,8},{8,9},{9,10},{10,1... | collective-permute-start | bytes 786440 | tf_op jit(solution)/shard_map/ppermute | solution.py:17
  67.5 25.6 %collective-permute-start.3 = (bf16[2,512,128]{2,1,0:T(8,128)(2,1)S(1)}, bf16[2,512,128]{2,1,0:T(8,128)(2,1)}, u32[]{:S(2)}, u32[]{:S(2)}) collective-permute-start(bf16[2,512,128]{2,1,0:T(8,128)(2,1)S(1)} %bitcast.342), channel_id=1, source_target_pairs={{1,0},{2,1},{3,2},{4,3},{5,4},{6,5},{7,6},{8,7},{9,8},{10,9},{11,1... | collective-permute-start | bytes 786440 | tf_op jit(solution)/shard_map/ppermute | solution.py:19
  70.1 4.6 %copy-start.6 = (bf16[2,8,8,8,384]{4,3,2,1,0:T(8,128)(2,1)S(1)}, bf16[2,8,8,8,384]{4,3,2,1,0:T(8,128)(2,1)}, u32[]{:S(2)}) copy-start(bf16[2,8,8,8,384]{4,3,2,1,0:T(8,128)(2,1)} %copy-done.5) | copy-start | bytes 2359300
  (57 other events, 89.8 us)
Sparse Core Ops, SparseCore 0:
  92.0 100.5 all-reduce.4
where the time goes:
time: 205 us; the launch traced here: 203 us
  local copies, waits for them, and re-layouts  81 us (40%)
  waiting for transfers between devices  59.1 us (29%)
  matrix products  20.4 us (10%)
  between operations  15.9 us (8%)
  other arithmetic  15.5 us (8%)
  starting transfers between devices  11.2 us (5%)
    psum x1, waiting for transfers between devices, local(): lax.psum((kernel_term, coarse_contribution), 'morton')  59.1 us
    gather x90, local copies, waits for them, and re-layouts, build_padded(): pieces.append(slab[positions[:, z_off * 9 + y_off * 3 + x_off]])  35.2 us
    dot_general x9, matrix products, weight_terms(): lax.dot_general(window.reshape(-1, 3 * channels), output_gradient, (((0,)...  10.6 us
    dot_general x9, local copies, waits for them, and re-layouts, weight_terms(): lax.dot_general(window.reshape(-1, 3 * channels), output_gradient, (((0,)...  10.3 us
    unnamed x178, local copies, waits for them, and re-layouts  9.49 us
    ppermute x2, starting transfers between devices, padded_2(): lax.ppermute(tail, axis, [(i, (i + 1) % count) for i in range(ends)])  8.39 us
    slice x46, local copies, waits for them, and re-layouts, build_padded(): slab = source[:, zlo:zhi, ylo:yhi, xlo:xhi, :]  7.85 us
  transfers between devices with their start and end apart: 5, of which 1 were waited for; matrix products, arithmetic and copies ran while one was open for 37% of the time, Pallas kernels for 0%

commit v1 on v0

v1 whole, which is shorter than its diff:
```python
import functools

import jax
import jax.numpy as jnp
from jax import lax
from jax.experimental import pallas as pl
from jax.experimental.pallas import tpu as pltpu
from jax.sharding import PartitionSpec as P

MESH = pl.DeviceIdType.MESH
F32 = jnp.float32
BF16 = jnp.bfloat16
PIECES = 16
STAGES = 4
ORDERS = ((0, 1, 2, 3), (0, 2, 3, 1), (0, 1, 2, 3))


def bit(value, place):
    return (value // (1 << place)) % 2


def put_plane(rows_of, target, brick, plane):
    columns = [
        jnp.concatenate([rows_of(0, dx), rows_of(1, dx), rows_of(2, dx)], axis=0)
        for dx in range(3)
    ]
    at = lax.broadcasted_iota(jnp.int32, columns[1].shape, 1)
    shifted = (
        pltpu.roll(jnp.where(at == 7, columns[0], columns[1]), 1, 1),
        columns[1],
        pltpu.roll(jnp.where(at == 0, columns[2], columns[1]), 7, 1),
    )
    for dx in range(3):
        flat = shifted[dx].reshape(80, 128)
        for dy in range(3):
            lane = (3 * dy + dx) * 128
            target[brick, plane, :, lane : lane + 128] = flat[8 * dy : 8 * dy + 64].astype(BF16)


ROWS = (slice(7, 8), slice(0, 8), slice(0, 1))


def inner_planes(own, target, brick, index):
    @pl.loop(0, 8)
    def _(z):
        def rows_of(dy, dx):
            return own[index[9 + 3 * dy + dx], z, ROWS[dy]]

        put_plane(rows_of, target, brick, z + 1)


def edge_planes(top, bottom, target, brick, index):
    def rows_top(dy, dx):
        return top[index[3 * dy + dx], ROWS[dy]]

    def rows_bottom(dy, dx):
        return bottom[index[18 + 3 * dy + dx], ROWS[dy]]

    put_plane(rows_top, target, brick, 0)
    put_plane(rows_bottom, target, brick, 9)


def body(n, factor, links, parents, feat, cot, coarse, kern, cweight,
         gi_out, gk_out, gc_out,
         own, top, bottom, halo, slope, slope_halo, p9, s9, kt, up, slcat, *rest):
    accs, gaths = rest[0:3], rest[3:6]
    recvs = [rest[6 + 4 * c : 10 + 4 * c] for c in range(3)]
    extra_recvs = rest[18:21]
    send_sem, recv_sem, halo_send, halo_recv = rest[21:25]
    bricks = feat.shape[0]
    coarse_bricks = coarse.shape[0]
    me = lax.axis_index("morton")
    group = lax.axis_index("groups")
    after, before = (me + 1) % n, (me + n - 1) % n
    bits = n.bit_length() - 1
    partners = [me + (1 - 2 * bit(me, b)) * (1 << b) for b in range(bits)]

    barrier = pltpu.get_barrier_semaphore()
    for other in [after, before] + partners:
        pl.semaphore_signal(barrier, inc=1, device_id=(group, other), device_id_type=MESH)
    pl.semaphore_wait(barrier, 2 + bits)

    def send(source, dest, other, s_sem, r_sem):
        copy = pltpu.make_async_remote_copy(
            src_ref=source, dst_ref=dest, send_sem=s_sem, recv_sem=r_sem,
            device_id=(group, other), device_id_type=MESH,
        )
        copy.start()
        return copy

    copies = []

    def exchange_halo(source, dest, which):
        pair = [
            send(source.at[:, pl.ds(448, 64)], dest.at[0], after,
                 halo_send.at[which, 0], halo_recv.at[which, 0]),
            send(source.at[:, pl.ds(0, 64)], dest.at[1], before,
                 halo_send.at[which, 1], halo_recv.at[which, 1]),
        ]
        copies.extend(pair)
        return pair

    def take_halo(pair, dest):
        for side, copy in enumerate(pair):
            copy.wait_recv()
        for b in range(bricks):
            top[b] = dest[0, b].astype(F32).reshape(8, 8, 128)
            bottom[bricks + b] = dest[1, b].astype(F32).reshape(8, 8, 128)

    def set_own(b, cells):
        own[b] = cells
        top[bricks + b] = cells[7]
        bottom[b] = cells[0]

    pair = exchange_halo(feat, halo, 0)

    index = []
    for b in range(bricks):
        row = []
        for o in range(27):
            link = links[b, o]
            if o < 9:
                spot, spare = link - (me - 1) * bricks, 2 * bricks
            elif o < 18:
                spot, spare = link - me * bricks, bricks
            else:
                spot, spare = link - me * bricks, 2 * bricks
            row.append(jnp.where(link < 0, spare, jnp.clip(spot, 0, spare)))
        index.append(row)

    own[bricks] = jnp.zeros((8, 8, 8, 128), F32)
    top[2 * bricks] = jnp.zeros((8, 8, 128), F32)
    bottom[2 * bricks] = jnp.zeros((8, 8, 128), F32)
    for b in range(bricks):
        set_own(b, feat[b].astype(F32).reshape(8, 8, 8, 128))
    for b in range(bricks):
        inner_planes(own, p9, b, index[b])

    row_at = lax.broadcasted_iota(jnp.int32, (64, 64), 0)
    col_at = lax.broadcasted_iota(jnp.int32, (64, 64), 1)
    for b in range(bricks):
        slot = parents[b]
        octant = slot % 8
        parent = jnp.clip(slot // 8 - me * coarse_bricks, 0, coarse_bricks - 1)
        oz, oy, ox = octant // 4, (octant // 2) % 2, octant % 2
        wanted = (4 * oy + row_at // 16) * 8 + 4 * ox + (row_at % 8) // 2
        pick = jnp.where(col_at == wanted, 1.0, 0.0).astype(BF16)
        for zc in range(4):
            cells = coarse[parent, 4 * oz + zc]
            spread = jnp.dot(pick, cells, preferred_element_type=F32).astype(BF16)
            up[b, 2 * zc] = spread
            up[b, 2 * zc + 1] = spread

    for o in range(27):
        lane = (o % 9) * 128
        mirror = 26 - o
        kt[o // 9, :, lane : lane + 128] = kern[mirror // 9, (mirror % 9) * 128 : (mirror % 9) * 128 + 128, :]

    blank = jnp.zeros((64, 128), BF16)
    for b in range(bricks):
        for dz in range(3):
            for plane in list(range(dz)) + list(range(8 + dz, 10)):
                slcat[b, plane, :, dz * 128 : dz * 128 + 128] = blank

    take_halo(pair, halo)
    for b in range(bricks):
        edge_planes(top, bottom, p9, b, index[b])

    for b in range(bricks):
        total = jnp.dot(up[b].reshape(512, 256), cweight[...], preferred_element_type=F32)
        for dz in range(3):
            total = total + jnp.dot(
                p9[b, dz : dz + 8].reshape(512, 1152), kern[dz], preferred_element_type=F32
            )
        gate = jax.nn.sigmoid(total)
        grads = cot[b].astype(F32)
        value = (grads * gate * (1.0 + total * (1.0 - gate))).astype(BF16)
        slope[b] = value
        for dz in range(3):
            slcat[b, dz : dz + 8, :, dz * 128 : dz * 128 + 128] = value.reshape(8, 64, 128)

    slope_pair = exchange_halo(slope, slope_halo, 1)

    def reduce_chunk(c):
        order = ORDERS[c]
        acc, gath, recv, sem = accs[c], gaths[c], recvs[c], 0
        digits = [bit(me, b) for b in order]
        bases = [0]
        for k in range(STAGES):
            bases.append(bases[k] + digits[k] * (PIECES >> (k + 1)))
        for k in range(STAGES):
            half = PIECES >> (k + 1)
            away = bases[k] + (1 - digits[k]) * half
            copy = send(acc.at[pl.ds(away, half)], recv[k], partners[order[k]],
                        send_sem.at[c, sem], recv_sem.at[c, sem])
            copies.append(copy)
            sem += 1
            yield
            copy.wait_recv()
            acc[pl.ds(bases[k + 1], half)] = acc[pl.ds(bases[k + 1], half)] + recv[k][...]
        mine = bases[STAGES]
        for e in range(STAGES, bits):
            copy = send(acc.at[pl.ds(mine, 1)], extra_recvs[c].at[pl.ds(e - STAGES, 1)],
                        partners[e], send_sem.at[c, sem], recv_sem.at[c, sem])
            sem += 1
            yield
            copy.wait()
            acc[pl.ds(mine, 1)] = acc[pl.ds(mine, 1)] + extra_recvs[c][pl.ds(e - STAGES, 1)]
        gath[pl.ds(mine, 1)] = acc[pl.ds(mine, 1)] * factor
        for k in reversed(range(STAGES)):
            half = PIECES >> (k + 1)
            span = pl.ds(bases[k + 1], half)
            copy = send(gath.at[span], gath.at[span], partners[order[k]],
                        send_sem.at[c, sem], recv_sem.at[c, sem])
            copies.append(copy)
            sem += 1
            yield
            copy.wait_recv()
        total = gath[:, :72, :].reshape(9, 128, 128)
        for dz in range(3):
            for dx in range(3):
                gk_out[9 * dz + 3 * c + dx] = total[3 * dz + dx]
        if c == 2:
            gc_out[...] = gath[:, 72:, :].reshape(256, 128)

    running = []

    def advance():
        for chunk in list(running):
            if next(chunk, "end") == "end":
                running.remove(chunk)

    contract_rows = (((0,), (0,)), ((), ()))
    contract_lanes = (((1,), (1,)), ((), ()))
    wide = slcat[...].reshape(bricks * 640, 384)
    for dy in range(3):
        term = lax.dot_general(
            p9[:, :, :, dy * 384 : dy * 384 + 384].reshape(bricks * 640, 384), wide,
            contract_rows, preferred_element_type=F32,
        )
        stacked = jnp.concatenate([term[:, dz * 128 : dz * 128 + 128] for dz in range(3)], axis=0)
        accs[dy][:, :72, :] = stacked.reshape(PIECES, 72, 128)
        if dy == 2:
            term = lax.dot_general(
                up[...].reshape(bricks * 512, 256), slope[...].reshape(bricks * 512, 128),
                contract_rows, preferred_element_type=F32,
            )
            accs[2][:, 72:, :] = term.reshape(PIECES, 16, 128)
        running.append(reduce_chunk(dy))
        next(running[-1])

    for b in range(bricks):
        set_own(b, slope[b].astype(F32).reshape(8, 8, 8, 128))
    for b in range(bricks):
        inner_planes(own, s9, b, index[b])
        advance()
    take_halo(slope_pair, slope_halo)
    for b in range(bricks):
        edge_planes(top, bottom, s9, b, index[b])
    for b in range(bricks):
        total = jnp.zeros((512, 128), F32)
        for dz in range(3):
            total = total + lax.dot_general(
                s9[b, dz : dz + 8].reshape(512, 1152), kt[dz], contract_lanes,
                preferred_element_type=F32,
            )
        gi_out[b] = total.astype(BF16)
        advance()
    while running:
        advance()
    for copy in copies:
        copy.wait_send()


def local(n, features, cotangent, coarse, kernel, coarse_weight, brick_links, parent_slot):
    bricks = features.shape[0]
    bits = n.bit_length() - 1
    factor = (bricks * 512 * n) ** (-0.5)
    heights = (72, 72, 88)
    vmem = pltpu.VMEM
    scratch = [
        vmem((bricks + 1, 8, 8, 8, 128), F32),
        vmem((2 * bricks + 1, 8, 8, 128), F32),
        vmem((2 * bricks + 1, 8, 8, 128), F32),
        vmem((2, bricks, 64, 128), BF16),
        vmem((bricks, 512, 128), BF16),
        vmem((2, bricks, 64, 128), BF16),
        vmem((bricks, 10, 64, 1152), BF16),
        vmem((bricks, 10, 64, 1152), BF16),
        vmem((3, 128, 1152), BF16),
        vmem((bricks, 8, 64, 256), BF16),
        vmem((bricks, 10, 64, 384), BF16),
    ]
    scratch += [vmem((PIECES, h, 128), F32) for h in heights]
    scratch += [vmem((PIECES, h, 128), F32) for h in heights]
    for h in heights:
        scratch += [vmem((PIECES >> (k + 1), h, 128), F32) for k in range(STAGES)]
    scratch += [vmem((max(bits - STAGES, 1), h, 128), F32) for h in heights]
    steps = STAGES + bits
    dma = pltpu.SemaphoreType.DMA
    scratch += [dma((3, steps)), dma((3, steps)), dma((2, 2)), dma((2, 2))]
    in_vmem = pl.BlockSpec(memory_space=pltpu.VMEM)
    in_smem = pl.BlockSpec(memory_space=pltpu.SMEM)
    return pl.pallas_call(
        functools.partial(body, n, factor),
        out_shape=(
            jax.ShapeDtypeStruct(features.shape, BF16),
            jax.ShapeDtypeStruct((27, 128, 128), F32),
            jax.ShapeDtypeStruct((256, 128), F32),
        ),
        in_specs=[in_smem, in_smem] + [in_vmem] * 5,
        out_specs=(in_vmem, in_vmem, in_vmem),
        scratch_shapes=scratch,
        compiler_params=pltpu.CompilerParams(
            collective_id=0, has_side_effects=True, vmem_limit_bytes=48 * 1024 * 1024
        ),
        cost_estimate=pl.CostEstimate(flops=3_000_000_000, bytes_accessed=8_000_000, transcendentals=0),
    )(brick_links, parent_slot, features, cotangent,
      coarse.reshape(coarse.shape[0], 8, 64, 256), kernel.reshape(3, 1152, 128), coarse_weight)


def solution(mesh):
    return jax.shard_map(
        functools.partial(local, mesh.shape["morton"]),
        mesh=mesh,
        in_specs=(
            P(("groups", "morton"), None, None),
            P(("groups", "morton"), None, None),
            P(("groups", "morton"), None, None),
            P(),
            P(),
            P(("groups", "morton"), None),
            P(("groups", "morton")),
        ),
        out_specs=(P(("groups", "morton"), None, None), P("groups", None, None), P("groups", None)),
        check_vma=False,
    )
```

time: 205 us -> 56 us (0.27)
  local copies, waits for them, and re-layouts: 81 us -> 9.02 us
  waiting for transfers between devices: 59.1 us -> 0 us
  Pallas kernels: 0 us -> 45.7 us
  matrix products: 20.4 us -> 0 us
  other arithmetic: 15.5 us -> 0 us
  between operations: 15.9 us -> 0.66 us
  starting transfers between devices: 11.2 us -> 0 us
    psum x1 -> x0, waiting for transfers between devices: 59.1 us -> none  [local(): lax.psum((kernel_term, coarse_contribution), 'morton')]
    pallas_call x0 -> x1, Pallas kernels: none -> 45.7 us  [local(): pl.pallas_call(functools.partial(body, n, factor), out_shape=(jax.ShapeDt...]
    gather x92 -> x0, local copies, waits for them, and re-layouts: 38.1 us -> none  [the longest x90 35.2 us: build_padded(): pieces.append(slab[positions[:, z_off * 9 + y_off * 3 + x_off]])]
    dot_general x29 -> x0, matrix products: 20.4 us -> none  [the longest x9 10.6 us: weight_terms(): lax.dot_general(window.reshape(-1, 3 * channels), output_gradient, (((0,)...]
    slice x56 -> x0, local copies, waits for them, and re-layouts: 18.6 us -> none  [the longest x46 7.85 us: build_padded(): slab = source[:, zlo:zhi, ylo:yhi, xlo:xhi, :]]
    ppermute x4 -> x0, starting transfers between devices: 11.1 us -> none  [the longest x2 8.39 us: padded_2(): lax.ppermute(tail, axis, [(i, (i + 1) % count) for i in range(ends)])]
    dot_general x10 -> x0, local copies, waits for them, and re-layouts: 10.6 us -> none  [the longest x9 10.3 us: weight_terms(): lax.dot_general(window.reshape(-1, 3 * channels), output_gradient, (((0,)...]
    concatenate x30 -> x0, other arithmetic: 7.03 us -> none  [the longest x4 1.71 us: build_padded(): return jnp.concatenate(planes, axis=1)]
  transfers between devices with their start and end apart: 5 -> 0, of which waited for: 1 -> 0; matrix products, arithmetic and copies ran while one was open for 37% -> 0% of each run, Pallas kernels for 0% -> 0%
where the time goes in v1:
time: 56 us; the launch traced here: 55.3 us
  Pallas kernels  45.7 us (82%)
  local copies, waits for them, and re-layouts  9.02 us (16%)
  between operations  0.66 us (1%)
    pallas_call x1, Pallas kernels, local(): pl.pallas_call(functools.partial(body, n, factor), out_shape=(jax.ShapeDt...  45.7 us
    unnamed x17, local copies, waits for them, and re-layouts  9.02 us

profile of v1, /device:TPU:0, one launch (start us, length us, event | category | flops | bytes accessed | tf_op | source)
XLA Modules:
  0.0 55.3 jit_solution(9416487723759998506)
XLA Ops:
  0.6 0.0 copy-start
  0.6 1.2 %copy-done = bf16[4,512,256]{2,1,0:T(8,128)(2,1)S(1)} copy-done((bf16[4,512,256]{2,1,0:T(8,128)(2,1)S(1)}, bf16[4,512,256]{2,1,0:T(8,128)(2,1)}, u32[]{:S(2)}) %copy-start) | copy-done | bytes 1048600
  1.9 0.0 copy-start.1
  1.9 1.2 %copy-done.1 = bf16[27,128,128]{2,1,0:T(8,128)(2,1)S(1)} copy-done((bf16[27,128,128]{2,1,0:T(8,128)(2,1)S(1)}, bf16[27,128,128]{2,1,0:T(8,128)(2,1)}, u32[]{:S(2)}) %copy-start.1) | copy-done | bytes 884760
  3.0 0.0 copy-start.2
  3.0 0.9 %copy-done.2 = bf16[2,512,128]{2,1,0:T(8,128)(2,1)S(1)} copy-done((bf16[2,512,128]{2,1,0:T(8,128)(2,1)S(1)}, bf16[2,512,128]{2,1,0:T(8,128)(2,1)}, u32[]{:S(2)}) %copy-start.2) | copy-done | bytes 262168
  4.0 0.0 copy-start.3
  4.0 0.9 %copy-done.3 = bf16[2,512,128]{2,1,0:T(8,128)(2,1)S(1)} copy-done((bf16[2,512,128]{2,1,0:T(8,128)(2,1)S(1)}, bf16[2,512,128]{2,1,0:T(8,128)(2,1)}, u32[]{:S(2)}) %copy-start.3) | copy-done | bytes 262168
  4.9 0.0 copy-start.4
  4.9 0.8 %copy-done.4 = bf16[256,128]{1,0:T(8,128)(2,1)S(1)} copy-done((bf16[256,128]{1,0:T(8,128)(2,1)S(1)}, bf16[256,128]{1,0:T(8,128)(2,1)}, u32[]{:S(2)}) %copy-start.4) | copy-done | bytes 65560
  5.8 0.0 copy-start.5
  5.8 0.7 %copy-done.5 = s32[2,27]{1,0:T(2,128)S(1)} copy-done((s32[2,27]{1,0:T(2,128)S(1)}, s32[2,27]{1,0:T(2,128)}, u32[]{:S(2)}) %copy-start.5) | copy-done | bytes 240
  6.4 0.0 copy-start.6
  6.4 0.7 %copy-done.6 = s32[2]{0:T(128)S(1)} copy-done((s32[2]{0:T(128)S(1)}, s32[2]{0:T(128)}, u32[]{:S(2)}) %copy-start.6) | copy-done | bytes 32
  7.1 45.7 %shard_map.94 = (bf16[2,512,128]{2,1,0:T(8,128)(2,1)S(1)}, f32[27,128,128]{2,1,0:T(8,128)S(1)}, f32[256,128]{1,0:T(8,128)S(1)}) custom-call(s32[2,27]{1,0:T(2,128)S(1)} %copy-done.5, s32[2]{0:T(128)S(1)} %copy-done.6, bf16[2,512,128]{2,1,0:T(8,128)(2,1)S(1)} %copy-done.2, bf16[2,512,128]{2,1,0:T(8,128)(2,1)S(1)} %copy-done.3, ...), custom_call_target="tpu_custom_call" | custom-call | flops 3000000000 | bytes 8000000 | tf_op jit(solution)/shard_map/pallas_call | solution.py:304
  52.8 0.7 %copy.13 = bf16[2,512,128]{2,1,0:T(8,128)(2,1)} copy(bf16[2,512,128]{2,1,0:T(8,128)(2,1)S(1)} %get-tuple-element.6) | data formatting | bytes 524288
  53.5 1.2 %copy.14 = f32[27,128,128]{2,1,0:T(8,128)} copy(f32[27,128,128]{2,1,0:T(8,128)S(1)} %get-tuple-element.7) | data formatting | bytes 3538944
  54.7 0.7 %copy.15 = f32[256,128]{1,0:T(8,128)} copy(f32[256,128]{1,0:T(8,128)S(1)} %get-tuple-element.8) | data formatting | bytes 262144
Async XLA Ops:
  0.6 1.2 %copy-start = (bf16[4,512,256]{2,1,0:T(8,128)(2,1)S(1)}, bf16[4,512,256]{2,1,0:T(8,128)(2,1)}, u32[]{:S(2)}) copy-start(bf16[4,512,256]{2,1,0:T(8,128)(2,1)} %param.9) | copy-start | bytes 3145732
  1.9 1.2 %copy-start.1 = (bf16[27,128,128]{2,1,0:T(8,128)(2,1)S(1)}, bf16[27,128,128]{2,1,0:T(8,128)(2,1)}, u32[]{:S(2)}) copy-start(bf16[27,128,128]{2,1,0:T(8,128)(2,1)} %param.10) | copy-start | bytes 2654212
  3.0 0.9 %copy-start.2 = (bf16[2,512,128]{2,1,0:T(8,128)(2,1)S(1)}, bf16[2,512,128]{2,1,0:T(8,128)(2,1)}, u32[]{:S(2)}) copy-start(bf16[2,512,128]{2,1,0:T(8,128)(2,1)} %feat.1) | copy-start | bytes 786436
  4.0 0.9 %copy-start.3 = (bf16[2,512,128]{2,1,0:T(8,128)(2,1)S(1)}, bf16[2,512,128]{2,1,0:T(8,128)(2,1)}, u32[]{:S(2)}) copy-start(bf16[2,512,128]{2,1,0:T(8,128)(2,1)} %cot.1) | copy-start | bytes 786436
  4.9 0.8 %copy-start.4 = (bf16[256,128]{1,0:T(8,128)(2,1)S(1)}, bf16[256,128]{1,0:T(8,128)(2,1)}, u32[]{:S(2)}) copy-start(bf16[256,128]{1,0:T(8,128)(2,1)} %cweight.1) | copy-start | bytes 196612
  5.8 0.7 %copy-start.5 = (s32[2,27]{1,0:T(2,128)S(1)}, s32[2,27]{1,0:T(2,128)}, u32[]{:S(2)}) copy-start(s32[2,27]{1,0:T(2,128)} %links.1) | copy-start | bytes 652
  6.4 0.7 %copy-start.6 = (s32[2]{0:T(128)S(1)}, s32[2]{0:T(128)}, u32[]{:S(2)}) copy-start(s32[2]{0:T(128)} %parents.1) | copy-start | bytes 28

commit v2 on v1

--- a/solution.py
+++ b/solution.py
@@ -13,6 +13,23 @@
 PIECES = 16
 STAGES = 4
 ORDERS = ((0, 1, 2, 3), (0, 2, 3, 1), (0, 1, 2, 3))
+LEVELS = 32000.0
+TINY = 2.0**-100
+
+
+def encode(values):
+    pieces = values.shape[0]
+    peak = jnp.maximum(jnp.max(jnp.abs(values), axis=1, keepdims=True), TINY)
+    power = jnp.ceil(jnp.log2(peak))
+    scaled = values * (jnp.exp2(-power) * LEVELS)
+    both = jnp.concatenate([scaled, jnp.broadcast_to(power, (pieces, 8, 128))], axis=1)
+    return jnp.floor(both + 0.5).astype(jnp.int32).astype(jnp.int16)
+
+
+def decode(codes):
+    rows = codes.shape[1] - 8
+    both = codes.astype(jnp.int32).astype(F32)
+    return both[:, :rows] * (jnp.exp2(both[:, rows : rows + 1]) * (1.0 / LEVELS))
 
 
 def bit(value, place):
@@ -60,10 +77,11 @@
     put_plane(rows_bottom, target, brick, 9)
 
 
-def body(n, factor, links, parents, feat, cot, coarse, kern, cweight,
-         gi_out, gk_out, gc_out,
+def body(n, factor, links_in, parents_in, feat_in, cot_in, coarse_in, kern_in, cweight_in,
+         gi_out, gath_a, gath_b, gath_c,
+         links, parents, feat, cot, coarse, kern, cweight, load_sem,
          own, top, bottom, halo, slope, slope_halo, p9, s9, kt, up, slcat, *rest):
-    accs, gaths = rest[0:3], rest[3:6]
+    accs, codes, gaths = rest[0:3], rest[3:6], (gath_a, gath_b, gath_c)
     recvs = [rest[6 + 4 * c : 10 + 4 * c] for c in range(3)]
     extra_recvs = rest[18:21]
     send_sem, recv_sem, halo_send, halo_recv = rest[21:25]
@@ -75,6 +93,15 @@
     bits = n.bit_length() - 1
     partners = [me + (1 - 2 * bit(me, b)) * (1 << b) for b in range(bits)]
 
+    sources = (links_in, parents_in, feat_in, kern_in, coarse_in, cweight_in, cot_in)
+    places = (links, parents, feat, kern, coarse, cweight, cot)
+    loads = [
+        pltpu.make_async_copy(source, place, load_sem.at[i])
+        for i, (source, place) in enumerate(zip(sources, places))
+    ]
+    for load in loads:
+        load.start()
+
     barrier = pltpu.get_barrier_semaphore()
     for other in [after, before] + partners:
         pl.semaphore_signal(barrier, inc=1, device_id=(group, other), device_id_type=MESH)
@@ -112,7 +139,9 @@
         top[bricks + b] = cells[7]
         bottom[b] = cells[0]
 
-    pair = exchange_halo(feat, halo, 0)
+    pair = exchange_halo(feat_in, halo, 0)
+    for load in loads[:3]:
+        load.wait()
 
     index = []
     for b in range(bricks):
@@ -136,6 +165,8 @@
     for b in range(bricks):
         inner_planes(own, p9, b, index[b])
 
+    for load in loads[3:]:
+        load.wait()
     row_at = lax.broadcasted_iota(jnp.int32, (64, 64), 0)
     col_at = lax.broadcasted_iota(jnp.int32, (64, 64), 1)
     for b in range(bricks):
@@ -191,13 +222,19 @@
         for k in range(STAGES):
             half = PIECES >> (k + 1)
             away = bases[k] + (1 - digits[k]) * half
-            copy = send(acc.at[pl.ds(away, half)], recv[k], partners[order[k]],
+            if k == 0:
+                source = acc.at[pl.ds(away, half)]
+            else:
+                source = codes[c].at[pl.ds(PIECES - 2 * half, half)]
+                source[...] = encode(acc[pl.ds(away, half)])
+            copy = send(source, recv[k], partners[order[k]],
                         send_sem.at[c, sem], recv_sem.at[c, sem])
             copies.append(copy)
             sem += 1
             yield
             copy.wait_recv()
-            acc[pl.ds(bases[k + 1], half)] = acc[pl.ds(bases[k + 1], half)] + recv[k][...]
+            other = recv[k][...] if k == 0 else decode(recv[k][...])
+            acc[pl.ds(bases[k + 1], half)] = acc[pl.ds(bases[k + 1], half)] + other
         mine = bases[STAGES]
         for e in range(STAGES, bits):
             copy = send(acc.at[pl.ds(mine, 1)], extra_recvs[c].at[pl.ds(e - STAGES, 1)],
@@ -206,7 +243,7 @@
             yield
             copy.wait()
             acc[pl.ds(mine, 1)] = acc[pl.ds(mine, 1)] + extra_recvs[c][pl.ds(e - STAGES, 1)]
-        gath[pl.ds(mine, 1)] = acc[pl.ds(mine, 1)] * factor
+        gath[pl.ds(mine, 1)] = encode(acc[pl.ds(mine, 1)] * factor)
         for k in reversed(range(STAGES)):
             half = PIECES >> (k + 1)
             span = pl.ds(bases[k + 1], half)
@@ -216,12 +253,6 @@
             sem += 1
             yield
             copy.wait_recv()
-        total = gath[:, :72, :].reshape(9, 128, 128)
-        for dz in range(3):
-            for dx in range(3):
-                gk_out[9 * dz + 3 * c + dx] = total[3 * dz + dx]
-        if c == 2:
-            gc_out[...] = gath[:, 72:, :].reshape(256, 128)
 
     running = []
 
@@ -272,13 +303,43 @@
         copy.wait_send()
 
 
+def finish(gi_in, gath_a, gath_b, gath_c, gi_out, gk_out, gc_out, gk, gc, sems):
+    first = pltpu.make_async_copy(gi_in, gi_out, sems.at[0])
+    first.start()
+    copies = [first]
+    for c, gath in enumerate((gath_a, gath_b, gath_c)):
+        values = decode(gath[...])
+        total = values[:, :72, :].reshape(3, 384, 128)
+        for dz in range(3):
+            gk[dz, c] = total[dz]
+        copy = pltpu.make_async_copy(gk.at[:, c], gk_out.at[:, c], sems.at[1 + c])
+        copy.start()
+        copies.append(copy)
+        if c == 2:
+            gc[...] = values[:, 72:, :].reshape(256, 128)
+    last = pltpu.make_async_copy(gc, gc_out, sems.at[4])
+    last.start()
+    for copy in copies + [last]:
+        copy.wait()
+
+
 def local(n, features, cotangent, coarse, kernel, coarse_weight, brick_links, parent_slot):
     bricks = features.shape[0]
     bits = n.bit_length() - 1
     factor = (bricks * 512 * n) ** (-0.5)
     heights = (72, 72, 88)
     vmem = pltpu.VMEM
+    tall = coarse.shape[0]
+    smem = pltpu.SMEM
     scratch = [
+        smem(brick_links.shape, jnp.int32),
+        smem(parent_slot.shape, jnp.int32),
+        vmem((bricks, 512, 128), BF16),
+        vmem((bricks, 512, 128), BF16),
+        vmem((tall, 8, 64, 256), BF16),
+        vmem((3, 1152, 128), BF16),
+        vmem((256, 128), BF16),
+        pltpu.SemaphoreType.DMA((7,)),
         vmem((bricks + 1, 8, 8, 8, 128), F32),
         vmem((2 * bricks + 1, 8, 8, 128), F32),
         vmem((2 * bricks + 1, 8, 8, 128), F32),
@@ -291,32 +352,46 @@
         vmem((bricks, 8, 64, 256), BF16),
         vmem((bricks, 10, 64, 384), BF16),
     ]
+    short = jnp.int16
     scratch += [vmem((PIECES, h, 128), F32) for h in heights]
-    scratch += [vmem((PIECES, h, 128), F32) for h in heights]
+    scratch += [vmem((PIECES, h + 8, 128), short) for h in heights]
     for h in heights:
-        scratch += [vmem((PIECES >> (k + 1), h, 128), F32) for k in range(STAGES)]
+        scratch += [vmem((PIECES // 2, h, 128), F32)]
+        scratch += [vmem((PIECES >> (k + 1), h + 8, 128), short) for k in range(1, STAGES)]
     scratch += [vmem((max(bits - STAGES, 1), h, 128), F32) for h in heights]
     steps = STAGES + bits
     dma = pltpu.SemaphoreType.DMA
     scratch += [dma((3, steps)), dma((3, steps)), dma((2, 2)), dma((2, 2))]
     in_vmem = pl.BlockSpec(memory_space=pltpu.VMEM)
-    in_smem = pl.BlockSpec(memory_space=pltpu.SMEM)
-    return pl.pallas_call(
+    in_hbm = pl.BlockSpec(memory_space=pltpu.HBM)
+    grad, gath_a, gath_b, gath_c = pl.pallas_call(
         functools.partial(body, n, factor),
-        out_shape=(
-            jax.ShapeDtypeStruct(features.shape, BF16),
-            jax.ShapeDtypeStruct((27, 128, 128), F32),
-            jax.ShapeDtypeStruct((256, 128), F32),
-        ),
-        in_specs=[in_smem, in_smem] + [in_vmem] * 5,
-        out_specs=(in_vmem, in_vmem, in_vmem),
+        out_shape=[jax.ShapeDtypeStruct(features.shape, BF16)]
+        + [jax.ShapeDtypeStruct((PIECES, h + 8, 128), short) for h in heights],
+        in_specs=[in_hbm] * 7,
+        out_specs=[in_vmem] * 4,
         scratch_shapes=scratch,
         compiler_params=pltpu.CompilerParams(
-            collective_id=0, has_side_effects=True, vmem_limit_bytes=48 * 1024 * 1024
+            collective_id=0, has_side_effects=True, vmem_limit_bytes=40 * 1024 * 1024
         ),
         cost_estimate=pl.CostEstimate(flops=3_000_000_000, bytes_accessed=8_000_000, transcendentals=0),
     )(brick_links, parent_slot, features, cotangent,
-      coarse.reshape(coarse.shape[0], 8, 64, 256), kernel.reshape(3, 1152, 128), coarse_weight)
+      coarse.reshape(tall, 8, 64, 256), kernel.reshape(3, 1152, 128), coarse_weight)
+    grad, grad_kernel, grad_coarse = pl.pallas_call(
+        finish,
+        out_shape=(
+            jax.ShapeDtypeStruct(features.shape, BF16),
+            jax.ShapeDtypeStruct((3, 3, 3 * 128, 128), F32),
+            jax.ShapeDtypeStruct((256, 128), F32),
+        ),
+        in_specs=[in_vmem] * 4,
+        out_specs=(in_hbm, in_hbm, in_hbm),
+        scratch_shapes=[
+            vmem((3, 3, 3 * 128, 128), F32), vmem((256, 128), F32), dma((5,)),
+        ],
+        compiler_params=pltpu.CompilerParams(vmem_limit_bytes=16 * 1024 * 1024),
+    )(grad, gath_a, gath_b, gath_c)
+    return grad, grad_kernel.reshape(27, 128, 128), grad_coarse
 
 
 def solution(mesh):

time: 56 us -> 47 us (0.84)
  Pallas kernels: 45.7 us -> 39.6 us
  local copies, waits for them, and re-layouts: 9.02 us -> 6.46 us
    pallas_call x1 -> x2, Pallas kernels: 45.7 us -> 39.6 us  [the longest x1 38.2 us: local(): pl.pallas_call(functools.partial(body, n, factor), out_shape=[jax.ShapeDt...]
    unnamed x17 -> x14, local copies, waits for them, and re-layouts: 9.02 us -> 6.46 us
where the time goes in v2:
time: 47 us; the launch traced here: 46.7 us
  Pallas kernels  39.6 us (84%)
  local copies, waits for them, and re-layouts  6.46 us (14%)
  between operations  0.66 us (1%)
    pallas_call x1, Pallas kernels, local(): pl.pallas_call(functools.partial(body, n, factor), out_shape=[jax.ShapeDt...  38.2 us
    unnamed x14, local copies, waits for them, and re-layouts  6.46 us
    pallas_call x1, Pallas kernels, local(): pl.pallas_call(finish, out_shape=(jax.ShapeDtypeStruct(features.shape, BF...  1.37 us

profile of v2, /device:TPU:0, one launch (start us, length us, event | category | flops | bytes accessed | tf_op | source)
XLA Modules:
  0.0 46.7 jit_solution(16507460749379511134)
XLA Ops:
  0.6 0.0 copy-start
  0.6 1.2 %copy-done = bf16[4,512,256]{2,1,0:T(8,128)(2,1)S(1)} copy-done((bf16[4,512,256]{2,1,0:T(8,128)(2,1)S(1)}, bf16[4,512,256]{2,1,0:T(8,128)(2,1)}, u32[]{:S(2)}) %copy-start) | copy-done | bytes 1048600
  1.9 0.0 copy-start.1
  1.9 1.2 %copy-done.1 = bf16[27,128,128]{2,1,0:T(8,128)(2,1)S(1)} copy-done((bf16[27,128,128]{2,1,0:T(8,128)(2,1)S(1)}, bf16[27,128,128]{2,1,0:T(8,128)(2,1)}, u32[]{:S(2)}) %copy-start.1) | copy-done | bytes 884760
  3.0 0.0 copy-start.2
  3.0 0.9 %copy-done.2 = bf16[2,512,128]{2,1,0:T(8,128)(2,1)S(1)} copy-done((bf16[2,512,128]{2,1,0:T(8,128)(2,1)S(1)}, bf16[2,512,128]{2,1,0:T(8,128)(2,1)}, u32[]{:S(2)}) %copy-start.2) | copy-done | bytes 262168
  4.0 0.0 copy-start.3
  4.0 0.9 %copy-done.3 = bf16[2,512,128]{2,1,0:T(8,128)(2,1)S(1)} copy-done((bf16[2,512,128]{2,1,0:T(8,128)(2,1)S(1)}, bf16[2,512,128]{2,1,0:T(8,128)(2,1)}, u32[]{:S(2)}) %copy-start.3) | copy-done | bytes 262168
  4.9 0.0 copy-start.4
  4.9 0.8 %copy-done.4 = bf16[256,128]{1,0:T(8,128)(2,1)S(1)} copy-done((bf16[256,128]{1,0:T(8,128)(2,1)S(1)}, bf16[256,128]{1,0:T(8,128)(2,1)}, u32[]{:S(2)}) %copy-start.4) | copy-done | bytes 65560
  5.8 0.0 copy-start.5
  5.8 0.7 %copy-done.5 = s32[2,27]{1,0:T(2,128)S(1)} copy-done((s32[2,27]{1,0:T(2,128)S(1)}, s32[2,27]{1,0:T(2,128)}, u32[]{:S(2)}) %copy-start.5) | copy-done | bytes 240
  6.4 0.0 copy-start.6
  6.4 0.7 %copy-done.6 = s32[2]{0:T(128)S(1)} copy-done((s32[2]{0:T(128)S(1)}, s32[2]{0:T(128)}, u32[]{:S(2)}) %copy-start.6) | copy-done | bytes 32
  7.1 38.2 %shard_map.94 = (bf16[2,512,128]{2,1,0:T(8,128)(2,1)S(1)}, s16[16,80,128]{2,1,0:T(8,128)(2,1)S(1)}, s16[16,80,128]{2,1,0:T(8,128)(2,1)S(1)}, s16[16,96,128]{2,1,0:T(8,128)(2,1)S(1)}) custom-call(s32[2,27]{1,0:T(2,128)S(1)} %copy-done.5, s32[2]{0:T(128)S(1)} %copy-done.6, bf16[2,512,128]{2,1,0:T(8,128)(2,1)S(1)} %copy-done.2, ...), custom_call_target="tpu_custom_call" | custom-call | flops 3000000000 | bytes 8000000 | tf_op jit(solution)/shard_map/pallas_call | solution.py:367
  45.3 1.4 %shard_map.95 = (bf16[2,512,128]{2,1,0:T(8,128)(2,1)}, f32[3,3,384,128]{3,2,1,0:T(8,128)}, f32[256,128]{1,0:T(8,128)}) custom-call(bf16[2,512,128]{2,1,0:T(8,128)(2,1)S(1)} %get-tuple-element.10.gi_in, s16[16,80,128]{2,1,0:T(8,128)(2,1)S(1)} %get-tuple-element.11.gath_a, s16[16,80,128]{2,1,0:T(8,128)(2,1)S(1)} %get-tuple-element.12.gath_b, ...), custom_call_target="tpu_custom_call" | custom-call | tf_op jit(solution)/shard_map/pallas_call | solution.py:380
Async XLA Ops:
  0.6 1.2 %copy-start = (bf16[4,512,256]{2,1,0:T(8,128)(2,1)S(1)}, bf16[4,512,256]{2,1,0:T(8,128)(2,1)}, u32[]{:S(2)}) copy-start(bf16[4,512,256]{2,1,0:T(8,128)(2,1)} %param.9) | copy-start | bytes 3145732
  1.9 1.2 %copy-start.1 = (bf16[27,128,128]{2,1,0:T(8,128)(2,1)S(1)}, bf16[27,128,128]{2,1,0:T(8,128)(2,1)}, u32[]{:S(2)}) copy-start(bf16[27,128,128]{2,1,0:T(8,128)(2,1)} %param.10) | copy-start | bytes 2654212
  3.0 0.9 %copy-start.2 = (bf16[2,512,128]{2,1,0:T(8,128)(2,1)S(1)}, bf16[2,512,128]{2,1,0:T(8,128)(2,1)}, u32[]{:S(2)}) copy-start(bf16[2,512,128]{2,1,0:T(8,128)(2,1)} %feat_in.1) | copy-start | bytes 786436
  4.0 0.9 %copy-start.3 = (bf16[2,512,128]{2,1,0:T(8,128)(2,1)S(1)}, bf16[2,512,128]{2,1,0:T(8,128)(2,1)}, u32[]{:S(2)}) copy-start(bf16[2,512,128]{2,1,0:T(8,128)(2,1)} %cot_in.1) | copy-start | bytes 786436
  4.9 0.8 %copy-start.4 = (bf16[256,128]{1,0:T(8,128)(2,1)S(1)}, bf16[256,128]{1,0:T(8,128)(2,1)}, u32[]{:S(2)}) copy-start(bf16[256,128]{1,0:T(8,128)(2,1)} %cweight_in.1) | copy-start | bytes 196612
  5.8 0.7 %copy-start.5 = (s32[2,27]{1,0:T(2,128)S(1)}, s32[2,27]{1,0:T(2,128)}, u32[]{:S(2)}) copy-start(s32[2,27]{1,0:T(2,128)} %links_in.1) | copy-start | bytes 652
  6.4 0.7 %copy-start.6 = (s32[2]{0:T(128)S(1)}, s32[2]{0:T(128)}, u32[]{:S(2)}) copy-start(s32[2]{0:T(128)} %parents_in.1) | copy-start | bytes 28

commit v3 on v2

--- a/solution.py
+++ b/solution.py
@@ -11,8 +11,8 @@
 F32 = jnp.float32
 BF16 = jnp.bfloat16
 PIECES = 16
-STAGES = 4
-ORDERS = ((0, 1, 2, 3), (0, 2, 3, 1), (0, 1, 2, 3))
+SPLIT_BITS = 4
+ORDERS = (((0,), (1,), (2, 3)), ((0,), (2, 3), (1,)), ((0,), (1,), (2, 3)))
 LEVELS = 32000.0
 TINY = 2.0**-100
 
@@ -34,6 +34,14 @@
 
 def bit(value, place):
     return (value // (1 << place)) % 2
+
+
+def stage_parts(order):
+    size, parts = PIECES, []
+    for group in order:
+        size >>= len(group)
+        parts.append((size, (1 << len(group)) - 1))
+    return parts
 
 
 def put_plane(rows_of, target, brick, plane):
@@ -82,16 +90,31 @@
          links, parents, feat, cot, coarse, kern, cweight, load_sem,
          own, top, bottom, halo, slope, slope_halo, p9, s9, kt, up, slcat, *rest):
     accs, codes, gaths = rest[0:3], rest[3:6], (gath_a, gath_b, gath_c)
-    recvs = [rest[6 + 4 * c : 10 + 4 * c] for c in range(3)]
-    extra_recvs = rest[18:21]
-    send_sem, recv_sem, halo_send, halo_recv = rest[21:25]
+    stages = len(ORDERS[0])
+    recvs = [rest[6 + stages * c : 6 + stages * (c + 1)] for c in range(3)]
+    extra_recvs = rest[6 + 3 * stages : 9 + 3 * stages]
+    send_sem, recv_sem, halo_send, halo_recv = rest[9 + 3 * stages :]
     bricks = feat.shape[0]
     coarse_bricks = coarse.shape[0]
     me = lax.axis_index("morton")
     group = lax.axis_index("groups")
     after, before = (me + 1) % n, (me + n - 1) % n
     bits = n.bit_length() - 1
-    partners = [me + (1 - 2 * bit(me, b)) * (1 << b) for b in range(bits)]
+
+    def partner(places):
+        other = me
+        for b in places:
+            other = other + (1 - 2 * bit(me, b)) * (1 << b)
+        return other
+
+    def toggles(group):
+        return [
+            [j for j in range(len(group)) if mask >> j & 1] for mask in range(1, 1 << len(group))
+        ]
+
+    partners = [
+        partner([group[j] for j in chosen]) for group in ORDERS[0] for chosen in toggles(group)
+    ] + [partner([b]) for b in range(SPLIT_BITS, bits)]
 
     sources = (links_in, parents_in, feat_in, kern_in, coarse_in, cweight_in, cot_in)
     places = (links, parents, feat, kern, coarse, cweight, cot)
@@ -105,7 +128,6 @@
     barrier = pltpu.get_barrier_semaphore()
     for other in [after, before] + partners:
         pl.semaphore_signal(barrier, inc=1, device_id=(group, other), device_id_type=MESH)
-    pl.semaphore_wait(barrier, 2 + bits)
 
     def send(source, dest, other, s_sem, r_sem):
         copy = pltpu.make_async_remote_copy(
@@ -139,7 +161,6 @@
         top[bricks + b] = cells[7]
         bottom[b] = cells[0]
 
-    pair = exchange_halo(feat_in, halo, 0)
     for load in loads[:3]:
         load.wait()
 
@@ -164,6 +185,8 @@
         set_own(b, feat[b].astype(F32).reshape(8, 8, 8, 128))
     for b in range(bricks):
         inner_planes(own, p9, b, index[b])
+    pl.semaphore_wait(barrier, 2 + len(partners))
+    pair = exchange_halo(feat_in, halo, 0)
 
     for load in loads[3:]:
         load.wait()
@@ -215,44 +238,63 @@
     def reduce_chunk(c):
         order = ORDERS[c]
         acc, gath, recv, sem = accs[c], gaths[c], recvs[c], 0
-        digits = [bit(me, b) for b in order]
+        parts = stage_parts(order)
+        digits = [
+            sum(bit(me, b) * (1 << (len(group) - 1 - j)) for j, b in enumerate(group)) for group in order
+        ]
         bases = [0]
-        for k in range(STAGES):
-            bases.append(bases[k] + digits[k] * (PIECES >> (k + 1)))
-        for k in range(STAGES):
-            half = PIECES >> (k + 1)
-            away = bases[k] + (1 - digits[k]) * half
-            if k == 0:
-                source = acc.at[pl.ds(away, half)]
-            else:
-                source = codes[c].at[pl.ds(PIECES - 2 * half, half)]
-                source[...] = encode(acc[pl.ds(away, half)])
-            copy = send(source, recv[k], partners[order[k]],
-                        send_sem.at[c, sem], recv_sem.at[c, sem])
-            copies.append(copy)
-            sem += 1
+        for digit, (size, _) in zip(digits, parts):
+            bases.append(bases[-1] + digit * size)
+        filled = 0
+        for k, (group, (size, _)) in enumerate(zip(order, parts)):
+            batch = []
+            for slot, chosen in enumerate(toggles(group)):
+                digit = digits[k]
+                for j in chosen:
+                    digit = digit + (1 - 2 * bit(me, group[j])) * (1 << (len(group) - 1 - j))
+                source = acc.at[pl.ds(bases[k] + digit * size, size)]
+                if k > 0:
+                    coded = codes[c].at[pl.ds(filled, size)]
+                    coded[...] = encode(source[...])
+                    source = coded
+                    filled += size
+                batch.append(
+                    send(source, recv[k].at[slot], partner([group[j] for j in chosen]),
+                         send_sem.at[c, sem], recv_sem.at[c, sem])
+                )
+                sem += 1
+            copies.extend(batch)
             yield
-            copy.wait_recv()
-            other = recv[k][...] if k == 0 else decode(recv[k][...])
-            acc[pl.ds(bases[k + 1], half)] = acc[pl.ds(bases[k + 1], half)] + other
-        mine = bases[STAGES]
-        for e in range(STAGES, bits):
-            copy = send(acc.at[pl.ds(mine, 1)], extra_recvs[c].at[pl.ds(e - STAGES, 1)],
-                        partners[e], send_sem.at[c, sem], recv_sem.at[c, sem])
+            span = pl.ds(bases[k + 1], size)
+            total = acc[span]
+            for slot, copy in enumerate(batch):
+                copy.wait_recv()
+                total = total + (recv[k][slot] if k == 0 else decode(recv[k][slot]))
+            acc[span] = total
+        mine = bases[-1]
+        for e in range(SPLIT_BITS, bits):
+            copy = send(acc.at[pl.ds(mine, 1)], extra_recvs[c].at[pl.ds(e - SPLIT_BITS, 1)],
+                        partner([e]), send_sem.at[c, sem], recv_sem.at[c, sem])
             sem += 1
             yield
             copy.wait()
-            acc[pl.ds(mine, 1)] = acc[pl.ds(mine, 1)] + extra_recvs[c][pl.ds(e - STAGES, 1)]
+            acc[pl.ds(mine, 1)] = acc[pl.ds(mine, 1)] + extra_recvs[c][pl.ds(e - SPLIT_BITS, 1)]
         gath[pl.ds(mine, 1)] = encode(acc[pl.ds(mine, 1)] * factor)
-        for k in reversed(range(STAGES)):
-            half = PIECES >> (k + 1)
-            span = pl.ds(bases[k + 1], half)
-            copy = send(gath.at[span], gath.at[span], partners[order[k]],
-                        send_sem.at[c, sem], recv_sem.at[c, sem])
-            copies.append(copy)
-            sem += 1
+        for k in reversed(range(len(order))):
+            group, (size, _) = order[k], parts[k]
+            span = pl.ds(bases[k + 1], size)
+            batch = []
+            for chosen in toggles(group):
+                batch.append(
+                    send(gath.at[span], gath.at[span], partner([group[j] for j in chosen]),
+                         send_sem.at[c, sem], recv_sem.at[c, sem])
+                )
+                sem += 1
+            copies.extend(batch)
             yield
-            copy.wait_recv()
+            for copy in batch:
+                copy.wait_recv()
+
 
     running = []
 
@@ -355,11 +397,12 @@
     short = jnp.int16
     scratch += [vmem((PIECES, h, 128), F32) for h in heights]
     scratch += [vmem((PIECES, h + 8, 128), short) for h in heights]
-    for h in heights:
-        scratch += [vmem((PIECES // 2, h, 128), F32)]
-        scratch += [vmem((PIECES >> (k + 1), h + 8, 128), short) for k in range(1, STAGES)]
-    scratch += [vmem((max(bits - STAGES, 1), h, 128), F32) for h in heights]
-    steps = STAGES + bits
+    for order, h in zip(ORDERS, heights):
+        for k, (size, others) in enumerate(stage_parts(order)):
+            rows, kind = (h, F32) if k == 0 else (h + 8, short)
+            scratch += [vmem((others, size, rows, 128), kind)]
+    scratch += [vmem((max(bits - SPLIT_BITS, 1), h, 128), F32) for h in heights]
+    steps = 2 * sum(others for _, others in stage_parts(ORDERS[0])) + bits - SPLIT_BITS
     dma = pltpu.SemaphoreType.DMA
     scratch += [dma((3, steps)), dma((3, steps)), dma((2, 2)), dma((2, 2))]
     in_vmem = pl.BlockSpec(memory_space=pltpu.VMEM)
@@ -372,7 +415,7 @@
         out_specs=[in_vmem] * 4,
         scratch_shapes=scratch,
         compiler_params=pltpu.CompilerParams(
-            collective_id=0, has_side_effects=True, vmem_limit_bytes=40 * 1024 * 1024
+            collective_id=0, has_side_effects=True, vmem_limit_bytes=60 * 1024 * 1024
         ),
         cost_estimate=pl.CostEstimate(flops=3_000_000_000, bytes_accessed=8_000_000, transcendentals=0),
     )(brick_links, parent_slot, features, cotangent,

time: 47 us -> 42.8 us (0.911)
  local copies, waits for them, and re-layouts: 6.46 us -> 3.88 us
  Pallas kernels: 39.6 us -> 38 us
    unnamed x14 -> x8, local copies, waits for them, and re-layouts: 6.46 us -> 3.88 us
    pallas_call x1, Pallas kernels: 38.2 us -> 36.6 us  [local(): pl.pallas_call(functools.partial(body, n, factor), out_shape=[jax.ShapeDt...]
where the time goes in v3:
time: 42.8 us; the launch traced here: 42.5 us
  Pallas kernels  38 us (89%)
  local copies, waits for them, and re-layouts  3.88 us (9%)
  between operations  0.65 us (2%)
    pallas_call x1, Pallas kernels, local(): pl.pallas_call(functools.partial(body, n, factor), out_shape=[jax.ShapeDt...  36.6 us
    unnamed x8, local copies, waits for them, and re-layouts  3.88 us
    pallas_call x1, Pallas kernels, local(): pl.pallas_call(finish, out_shape=(jax.ShapeDtypeStruct(features.shape, BF...  1.37 us

profile of v3, /device:TPU:0, one launch (start us, length us, event | category | flops | bytes accessed | tf_op | source)
XLA Modules:
  0.0 42.5 jit_solution(4746727198829623441)
XLA Ops:
  0.6 36.6 %shard_map.94 = (bf16[2,512,128]{2,1,0:T(8,128)(2,1)}, s16[16,80,128]{2,1,0:T(8,128)(2,1)}, s16[16,80,128]{2,1,0:T(8,128)(2,1)}, s16[16,96,128]{2,1,0:T(8,128)(2,1)}) custom-call(s32[2,27]{1,0:T(2,128)} %links_in.1, s32[2]{0:T(128)} %parents_in.1, bf16[2,512,128]{2,1,0:T(8,128)(2,1)} %feat_in.1, bf16[2,512,128]{2,1,0:T(8,128)(2,1)} %cot_in.1, ...), custom_call_target="tpu_custom_call" | custom-call | flops 3000000000 | bytes 8000000 | tf_op jit(solution)/shard_map/pallas_call | solution.py:410
  37.3 0.0 copy-start
  37.3 1.0 %copy-done = s16[16,96,128]{2,1,0:T(8,128)(2,1)S(1)} copy-done((s16[16,96,128]{2,1,0:T(8,128)(2,1)S(1)}, s16[16,96,128]{2,1,0:T(8,128)(2,1)}, u32[]{:S(2)}) %copy-start) | copy-done | bytes 393240
  38.3 0.0 copy-start.1
  38.3 1.0 %copy-done.1 = s16[16,80,128]{2,1,0:T(8,128)(2,1)S(1)} copy-done((s16[16,80,128]{2,1,0:T(8,128)(2,1)S(1)}, s16[16,80,128]{2,1,0:T(8,128)(2,1)}, u32[]{:S(2)}) %copy-start.1) | copy-done | bytes 327704
  39.2 0.0 copy-start.2
  39.2 1.0 %copy-done.2 = s16[16,80,128]{2,1,0:T(8,128)(2,1)S(1)} copy-done((s16[16,80,128]{2,1,0:T(8,128)(2,1)S(1)}, s16[16,80,128]{2,1,0:T(8,128)(2,1)}, u32[]{:S(2)}) %copy-start.2) | copy-done | bytes 327704
  40.2 0.0 copy-start.3
  40.2 0.9 %copy-done.3 = bf16[2,512,128]{2,1,0:T(8,128)(2,1)S(1)} copy-done((bf16[2,512,128]{2,1,0:T(8,128)(2,1)S(1)}, bf16[2,512,128]{2,1,0:T(8,128)(2,1)}, u32[]{:S(2)}) %copy-start.3) | copy-done | bytes 262168
  41.2 1.4 %shard_map.95 = (bf16[2,512,128]{2,1,0:T(8,128)(2,1)}, f32[3,3,384,128]{3,2,1,0:T(8,128)}, f32[256,128]{1,0:T(8,128)}) custom-call(bf16[2,512,128]{2,1,0:T(8,128)(2,1)S(1)} %copy-done.3, s16[16,80,128]{2,1,0:T(8,128)(2,1)S(1)} %copy-done.1, s16[16,80,128]{2,1,0:T(8,128)(2,1)S(1)} %copy-done.2, s16[16,96,128]{2,1,0:T(8,128)(2,1)S(1)} %copy-done), custom_call_target="tpu_custom_call" | custom-call | tf_op jit(solution)/shard_map/pallas_call | solution.py:423
Async XLA Ops:
  37.3 1.0 %copy-start = (s16[16,96,128]{2,1,0:T(8,128)(2,1)S(1)}, s16[16,96,128]{2,1,0:T(8,128)(2,1)}, u32[]{:S(2)}) copy-start(s16[16,96,128]{2,1,0:T(8,128)(2,1)} %get-tuple-element.13.gath_c) | copy-start | bytes 1179652
  38.3 1.0 %copy-start.1 = (s16[16,80,128]{2,1,0:T(8,128)(2,1)S(1)}, s16[16,80,128]{2,1,0:T(8,128)(2,1)}, u32[]{:S(2)}) copy-start(s16[16,80,128]{2,1,0:T(8,128)(2,1)} %get-tuple-element.11.gath_a) | copy-start | bytes 983044
  39.2 1.0 %copy-start.2 = (s16[16,80,128]{2,1,0:T(8,128)(2,1)S(1)}, s16[16,80,128]{2,1,0:T(8,128)(2,1)}, u32[]{:S(2)}) copy-start(s16[16,80,128]{2,1,0:T(8,128)(2,1)} %get-tuple-element.12.gath_b) | copy-start | bytes 983044
  40.2 0.9 %copy-start.3 = (bf16[2,512,128]{2,1,0:T(8,128)(2,1)S(1)}, bf16[2,512,128]{2,1,0:T(8,128)(2,1)}, u32[]{:S(2)}) copy-start(bf16[2,512,128]{2,1,0:T(8,128)(2,1)} %get-tuple-element.10.gi_in) | copy-start | bytes 786436

commit v4 on v3

--- a/solution.py
+++ b/solution.py
@@ -345,12 +345,22 @@
         copy.wait_send()
 
 
-def finish(gi_in, gath_a, gath_b, gath_c, gi_out, gk_out, gc_out, gk, gc, sems):
-    first = pltpu.make_async_copy(gi_in, gi_out, sems.at[0])
+def finish(gi_in, gath_a, gath_b, gath_c, gi_out, gk_out, gc_out,
+           here_gi, here_a, here_b, here_c, gk, gc, load_sems, sems):
+    sources, places = (gi_in, gath_a, gath_b, gath_c), (here_gi, here_a, here_b, here_c)
+    loads = [
+        pltpu.make_async_copy(source, place, load_sems.at[c])
+        for c, (source, place) in enumerate(zip(sources, places))
+    ]
+    for load in loads:
+        load.start()
+    loads[0].wait()
+    first = pltpu.make_async_copy(here_gi, gi_out, sems.at[0])
     first.start()
     copies = [first]
-    for c, gath in enumerate((gath_a, gath_b, gath_c)):
-        values = decode(gath[...])
+    for c, here in enumerate(places[1:]):
+        loads[c + 1].wait()
+        values = decode(here[...])
         total = values[:, :72, :].reshape(3, 384, 128)
         for dz in range(3):
             gk[dz, c] = total[dz]
@@ -427,12 +437,14 @@
             jax.ShapeDtypeStruct((3, 3, 3 * 128, 128), F32),
             jax.ShapeDtypeStruct((256, 128), F32),
         ),
-        in_specs=[in_vmem] * 4,
+        in_specs=[in_hbm] * 4,
         out_specs=(in_hbm, in_hbm, in_hbm),
         scratch_shapes=[
-            vmem((3, 3, 3 * 128, 128), F32), vmem((256, 128), F32), dma((5,)),
+            vmem(features.shape, BF16),
+            *[vmem((PIECES, h + 8, 128), short) for h in heights],
+            vmem((3, 3, 3 * 128, 128), F32), vmem((256, 128), F32), dma((4,)), dma((5,)),
         ],
-        compiler_params=pltpu.CompilerParams(vmem_limit_bytes=16 * 1024 * 1024),
+        compiler_params=pltpu.CompilerParams(vmem_limit_bytes=60 * 1024 * 1024),
     )(grad, gath_a, gath_b, gath_c)
     return grad, grad_kernel.reshape(27, 128, 128), grad_coarse
 

time: 42.8 us -> 39.9 us (0.932)
  local copies, waits for them, and re-layouts: 3.88 us -> 0 us
  Pallas kernels: 38 us -> 39.1 us
    unnamed x8 -> x0, local copies, waits for them, and re-layouts: 3.88 us -> none
    pallas_call x1, Pallas kernels: 1.37 us -> 2.44 us  [local(): pl.pallas_call(finish, out_shape=(jax.ShapeDtypeStruct(features.shape, BF...]
where the time goes in v4:
time: 39.9 us; the launch traced here: 39.7 us
  Pallas kernels  39.1 us (98%)
  between operations  0.64 us (2%)
    pallas_call x1, Pallas kernels, local(): pl.pallas_call(functools.partial(body, n, factor), out_shape=[jax.ShapeDt...  36.6 us
    pallas_call x1, Pallas kernels, local(): pl.pallas_call(finish, out_shape=(jax.ShapeDtypeStruct(features.shape, BF...  2.44 us

profile of v4, /device:TPU:0, one launch (start us, length us, event | category | flops | bytes accessed | tf_op | source)
XLA Modules:
  0.0 39.7 jit_solution(15061972195777910716)
XLA Ops:
  0.6 36.6 %shard_map.94 = (bf16[2,512,128]{2,1,0:T(8,128)(2,1)}, s16[16,80,128]{2,1,0:T(8,128)(2,1)}, s16[16,80,128]{2,1,0:T(8,128)(2,1)}, s16[16,96,128]{2,1,0:T(8,128)(2,1)}) custom-call(s32[2,27]{1,0:T(2,128)} %links_in.1, s32[2]{0:T(128)} %parents_in.1, bf16[2,512,128]{2,1,0:T(8,128)(2,1)} %feat_in.1, bf16[2,512,128]{2,1,0:T(8,128)(2,1)} %cot_in.1, ...), custom_call_target="tpu_custom_call" | custom-call | flops 3000000000 | bytes 8000000 | tf_op jit(solution)/shard_map/pallas_call | solution.py:420
  37.3 2.4 %shard_map.95 = (bf16[2,512,128]{2,1,0:T(8,128)(2,1)}, f32[3,3,384,128]{3,2,1,0:T(8,128)}, f32[256,128]{1,0:T(8,128)}) custom-call(bf16[2,512,128]{2,1,0:T(8,128)(2,1)} %get-tuple-element.10.gi_in, s16[16,80,128]{2,1,0:T(8,128)(2,1)} %get-tuple-element.11.gath_a, s16[16,80,128]{2,1,0:T(8,128)(2,1)} %get-tuple-element.12.gath_b, ...), custom_call_target="tpu_custom_call" | custom-call | tf_op jit(solution)/shard_map/pallas_call | solution.py:433
